TPU v7x, 256 devices: a whole 4x4x8 slice. The times are simulated.
256 devices in a mesh: frame: 16 (over x, z_hi, core), patch: 16 (over y, z_lo).
Axes of the slice: x: 4, y: 4, z: 8 (z_hi: 2, z_lo: 4; z = z_hi * 4 + z_lo), core: 2. Of those that a mesh axis runs over, the one named last changes fastest.
Arguments:
- latent: bfloat16 [32, 2048, 1536], P('frame', 'patch'), may hold values from -6 to 6
- timesteps: int32 [3], replicated, may hold values from 1 to 999
- w_qkv: bfloat16 [1536, 2304], replicated, may hold values from -2.5 to 2.5
- w_out: bfloat16 [768, 1536], replicated, may hold values from -0.21875 to 0.21875
- w_time: bfloat16 [256, 4608], replicated, may hold values from -0.75 to 0.75
- stale_kv: bfloat16 [32, 2048, 1536], P('frame', 'patch'), may hold values from -9 to 9
Outputs:
- latent_out: bfloat16 [32, 2048, 1536], P('frame', 'patch')
- velocity: bfloat16 [32, 2048, 1536], P('frame', 'patch')
- next_kv: bfloat16 [32, 2048, 1536], P('frame', 'patch')
All inputs are finite; a program needn't handle non-finite values.
Results may differ from a plain program's by a relative error of at most 0.028.
Values may be sent and summed in bfloat16 or wider, within the bound.
A program may use at most 128 MiB of HBM per device.

v0:
```python
import math

import jax
import jax.numpy as jnp
from jax import lax
from jax.sharding import PartitionSpec as P

HEAD_DIM = 128
SHEADS = 3
THEADS = 3
STEPS = 2


def sigma_level(index):
    unit = index.astype(jnp.float32) / 1000.0
    return 5.0 * unit / (1.0 + 4.0 * unit)


def modulation(index, w_time, model_width):
    level = sigma_level(index) * 1000.0
    half = w_time.shape[0] // 2
    freqs = jnp.exp(-math.log(10000.0) * jnp.arange(half, dtype=jnp.float32) / half)
    angles = level * freqs
    embed = jnp.concatenate([jnp.cos(angles), jnp.sin(angles)])
    mods = jnp.dot(
        jax.nn.silu(embed)[None, :], w_time.astype(jnp.float32), precision=lax.Precision.HIGHEST
    )[0]
    return (mods[:model_width], mods[model_width : 2 * model_width], mods[2 * model_width :])


def normalize(latent):
    value_rows = latent.astype(jnp.float32)
    center = jnp.mean(value_rows, axis=-1, keepdims=True)
    value_deviation = jnp.mean((value_rows - center) ** 2, axis=-1, keepdims=True)
    return (value_rows - center) / jnp.sqrt(value_deviation + 1e-06)


def softmax_rows(scores):
    top = jnp.max(scores, axis=-1, keepdims=True)
    expo = jnp.exp(scores - top)
    return (expo / jnp.sum(expo, axis=-1, keepdims=True)).astype(jnp.bfloat16)


def heads_of(block, heads):
    return block.reshape(block.shape[0], block.shape[1], heads, HEAD_DIM)


def spatial_attend(query, fresh, stale, base):
    swidth = SHEADS * HEAD_DIM
    gathered = lax.all_gather(stale, "patch", axis=1, tiled=True)
    keys_all = lax.dynamic_update_slice_in_dim(gathered, fresh, base, 1)
    queries = heads_of(query, SHEADS)
    keys = heads_of(keys_all[..., :swidth], SHEADS)
    value_rows = heads_of(keys_all[..., swidth:], SHEADS)
    scores = jnp.einsum(
        "fqhd,fkhd->fhqk", queries, keys, preferred_element_type=jnp.float32
    ) / math.sqrt(HEAD_DIM)
    weights = softmax_rows(scores)
    result = jnp.einsum("fhqk,fkhd->fqhd", weights, value_rows, preferred_element_type=jnp.float32)
    return result.reshape(query.shape[0], query.shape[1], swidth).astype(jnp.bfloat16)


def temporal_attend(query, fresh, stale, base):
    twidth = THEADS * HEAD_DIM
    gathered = lax.all_gather(stale, "frame", axis=0, tiled=True)
    keys_all = lax.dynamic_update_slice_in_dim(gathered, fresh, base, 0)
    queries = heads_of(query, THEADS)
    scores = jnp.einsum(
        "qphd,kphd->phqk",
        queries,
        heads_of(keys_all[..., :twidth], THEADS),
        preferred_element_type=jnp.float32,
    ) / math.sqrt(HEAD_DIM)
    weights = softmax_rows(scores)
    result = jnp.einsum(
        "phqk,kphd->qphd",
        weights,
        heads_of(keys_all[..., twidth:], THEADS),
        preferred_element_type=jnp.float32,
    )
    return result.reshape(query.shape[0], query.shape[1], twidth).astype(jnp.bfloat16)


def per_device(latent, timesteps, w_qkv, w_out, w_time, stale_kv):
    frames_dev, spatial_dev, model_width = latent.shape
    swidth = SHEADS * HEAD_DIM
    qwidth = w_out.shape[0]
    patch_base = lax.axis_index("patch") * spatial_dev
    frame_base = lax.axis_index("frame") * frames_dev
    current = latent
    previous = stale_kv
    for step in range(STEPS):
        shift, scale, gate = modulation(timesteps[step], w_time, model_width)
        dsig = sigma_level(timesteps[step + 1]) - sigma_level(timesteps[step])
        hidden = (normalize(current) * (1.0 + scale) + shift).astype(jnp.bfloat16)
        proj = jnp.dot(
            hidden.reshape(-1, model_width), w_qkv, preferred_element_type=jnp.float32
        ).astype(jnp.bfloat16)
        proj = proj.reshape(frames_dev, spatial_dev, -1)
        query = proj[..., :qwidth]
        fresh = proj[..., qwidth:]
        spatial_out = spatial_attend(
            query[..., :swidth], fresh[..., : 2 * swidth], previous[..., : 2 * swidth], patch_base
        )
        temporal_out = temporal_attend(
            query[..., swidth:], fresh[..., 2 * swidth :], previous[..., 2 * swidth :], frame_base
        )
        attended = jnp.concatenate([spatial_out, temporal_out], axis=-1)
        branch = jnp.dot(
            attended.reshape(-1, qwidth), w_out, preferred_element_type=jnp.float32
        ).reshape(frames_dev, spatial_dev, model_width)
        vel = gate * branch
        current = (current.astype(jnp.float32) + dsig * vel).astype(jnp.bfloat16)
        previous = fresh
    return (current, vel.astype(jnp.bfloat16), previous)


def solution(mesh):
    placed = (P("frame", "patch", None), P(), P(), P(), P(), P("frame", "patch", None))
    return jax.shard_map(
        per_device,
        mesh=mesh,
        in_specs=placed,
        out_specs=(P("frame", "patch", None), P("frame", "patch", None), P("frame", "patch", None)),
        check_vma=False,
    )
```

profile of v0, /device:TPU:1, one launch (start us, length us, event | category | flops | bytes accessed | tf_op | source)
XLA Modules:
  0.0 522.7 jit_solution(2416057228188662619)
XLA Ops:
  7.2 2.1 fusion.65
  9.4 0.9 copy.71
  12.4 2.7 convolution_reduce_fusion.1
  16.0 5.0 convolution_convert_fusion.1
  21.1 1.1 copy-done.5
  23.0 0.9 copy.72
  24.0 1.2 copy.74
  26.4 1.8 fusion.63
  28.3 1.8 copy.75
  30.1 1.7 copy.47
  31.8 1.7 copy.73
  33.7 2.7 convolution_reduce_fusion
  37.0 71.5 %all-gather.7.cloned.1.call-done = bf16[32,128,768]{2,1,0:T(8,128)(2,1)} async-done(((bf16[2,128,768]{2,1,0:T(8,128)(2,1)}), bf16[32,128,768]{2,1,0:T(8,128)(2,1)}) %all-gather.7.cloned.1.call-update) | async-done | bytes 6291472 | tf_op jit(solution)/shard_map/all_gather | solution.py:65
  108.5 8.6 %copy.45 = bf16[32,128,768]{1,2,0:T(8,128)(2,1)} copy(bf16[32,128,768]{2,1,0:T(8,128)(2,1)} %all-gather.7.cloned.1.call-done) | data formatting | bytes 12582912 | tf_op jit(solution)/shard_map/all_gather | solution.py:65
  117.1 0.8 constant_dynamic-update-slice_fusion.2
  117.9 6.2 %fusion.59 = (bf16[32,128,384]{1,2,0:T(8,128)(2,1)}, bf16[32,128,384]{1,2,0:T(8,128)(2,1)}) fusion(bf16[32,128,768]{1,2,0:T(8,128)(2,1)} %constant_dynamic-update-slice_fusion.2), kind=kLoop, calls=%fused_computation.91 | loop fusion | bytes 12582912 | tf_op jit(solution)/shard_map/slice | solution.py:71
  124.1 4.9 copy.49
  129.0 5.0 copy.48
  134.0 5.3 %fusion.67 = (f32[128,3,2]{2,1,0:T(4,128)}, f32[128,3,2,32]{3,2,1,0:T(2,128)}) fusion(bf16[2,128,3,128]{3,0,2,1:T(2,128)(2,1)S(1)} %copy-done.8, bf16[32,128,3,128]{3,0,2,1:T(8,128)(2,1)} %copy.48), kind=kOutput, calls=%fused_computation.99 | convolution fusion | flops 6365215 | bytes 3443712 | tf_op jit(solution)/shard_map/sub | solution.py:40
  139.3 3.8 fusion.32
  143.1 1.8 copy.50
  144.8 1.7 copy.52
  146.6 105.5 %all-gather.5.cloned.1.call-done = bf16[2,2048,768]{1,2,0:T(8,128)(2,1)} async-done(((bf16[2,128,768]{1,2,0:T(8,128)(2,1)}), bf16[2,2048,768]{1,2,0:T(8,128)(2,1)}) %all-gather.5.cloned.1.call-update) | async-done | bytes 6291472 | tf_op jit(solution)/shard_map/all_gather | solution.py:50
  252.1 0.9 constant_dynamic-update-slice_fusion.3
  253.0 6.6 %fusion.58 = (bf16[2,2048,384]{1,2,0:T(8,128)(2,1)}, bf16[2,2048,384]{1,2,0:T(8,128)(2,1)}) fusion(bf16[2,2048,768]{1,2,0:T(8,128)(2,1)} %constant_dynamic-update-slice_fusion.3), kind=kLoop, calls=%fused_computation.90 | loop fusion | bytes 12582912 | tf_op jit(solution)/shard_map/slice | solution.py:53
  259.6 6.6 %fusion.68 = (f32[2,3,128]{2,1,0:T(4,128)S(1)}, f32[2,3,128,2048]{3,2,1,0:T(8,128)}) fusion(bf16[2,128,3,128]{1,3,2,0:T(8,128)(2,1)S(1)} %bitcast.86, bf16[2,2048,3,128]{1,3,2,0:T(8,128)(2,1)} %bitcast.72), kind=kOutput, calls=%fused_computation.100 | convolution fusion | flops 407373824 | bytes 9636864 | tf_op jit(solution)/shard_map/sub | solution.py:40
  266.2 5.5 %fusion.31 = bf16[2,3,128,128]{3,2,1,0:T(8,128)(2,1)} fusion(bf16[2,2048,3,128]{1,3,2,0:T(8,128)(2,1)} %bitcast.77, f32[2,3,128,2048]{3,2,1,0:T(8,128)} %get-tuple-element.35, f32[2,3,128]{2,1,0:T(4,128)S(1)} %get-tuple-element.34), kind=kOutput, calls=%fused_computation.46 | convolution fusion | flops 405897216 | bytes 9636864 | tf_op jit(solution)/shard_map/fhqk,fkhd->fqhd/dot_general | solution.py:59
  271.7 1.1 copy.51
  272.8 1.6 fusion.69
  274.8 0.9 copy-done.1
  276.0 5.0 convolution_convert_fusion
  281.0 0.9 slice.152
  282.0 0.9 fusion.62
  282.9 1.9 copy.78
  284.8 67.6 %all-gather.11.cloned.1.call-done = bf16[32,128,768]{2,1,0:T(8,128)(2,1)} async-done(((bf16[2,128,768]{2,1,0:T(8,128)(2,1)}), bf16[32,128,768]{2,1,0:T(8,128)(2,1)}) %all-gather.11.cloned.1.call-update) | async-done | bytes 6291472 | tf_op jit(solution)/shard_map/all_gather | solution.py:65
  352.4 8.6 %copy.59 = bf16[32,128,768]{1,2,0:T(8,128)(2,1)} copy(bf16[32,128,768]{2,1,0:T(8,128)(2,1)} %all-gather.11.cloned.1.call-done) | data formatting | bytes 12582912 | tf_op jit(solution)/shard_map/all_gather | solution.py:65
  361.0 1.8 constant_dynamic-update-slice_fusion
  362.9 6.4 %fusion.57 = (bf16[32,128,384]{1,2,0:T(8,128)(2,1)}, bf16[32,128,384]{1,2,0:T(8,128)(2,1)}) fusion(bf16[32,128,768]{1,2,0:T(8,128)(2,1)} %constant_dynamic-update-slice_fusion), kind=kLoop, calls=%fused_computation.89 | loop fusion | bytes 12582912 | tf_op jit(solution)/shard_map/slice | solution.py:71
  369.2 4.9 copy.63
  374.9 1.1 copy.79
  376.2 5.0 copy.62
  381.2 4.6 fusion.70
  385.8 3.0 fusion.33
  389.3 104.2 %all-gather.9.cloned.1.call-done = bf16[2,2048,768]{1,2,0:T(8,128)(2,1)} async-done(((bf16[2,128,768]{1,2,0:T(8,128)(2,1)}), bf16[2,2048,768]{1,2,0:T(8,128)(2,1)}) %all-gather.9.cloned.1.call-update) | async-done | bytes 6291472 | tf_op jit(solution)/shard_map/all_gather | solution.py:50
  494.3 6.7 %fusion.56 = (bf16[2,2048,384]{1,2,0:T(8,128)(2,1)}, bf16[2,2048,384]{1,2,0:T(8,128)(2,1)}) fusion(bf16[2,2048,768]{1,2,0:T(8,128)(2,1)} %constant_dynamic-update-slice_fusion.1), kind=kLoop, calls=%fused_computation.88 | loop fusion | bytes 12582912 | tf_op jit(solution)/shard_map/slice | solution.py:53
  501.1 6.7 %fusion.71 = (f32[2,3,128]{2,1,0:T(4,128)S(1)}, f32[2,3,128,2048]{3,2,1,0:T(8,128)}) fusion(bf16[2,128,3,128]{1,3,2,0:T(8,128)(2,1)S(1)} %bitcast.87, bf16[2,2048,3,128]{1,3,2,0:T(8,128)(2,1)} %bitcast.71), kind=kOutput, calls=%fused_computation.103 | convolution fusion | flops 407373824 | bytes 9636864 | tf_op jit(solution)/shard_map/sub | solution.py:40
  507.8 4.8 fusion.30
  512.8 3.3 fusion.60
  (55 shorter events, 7.2 us)
Async XLA Ops:
  7.2 265.7 %copy-start = (bf16[768,1536]{1,0:T(8,128)(2,1)S(1)}, bf16[768,1536]{1,0:T(8,128)(2,1)}, u32[]{:S(2)}) copy-start(bf16[768,1536]{1,0:T(8,128)(2,1)} %param.9) | copy-start | bytes 7077892
  7.2 3.2 copy-start.11
  7.2 4.6 copy-start.2
  7.2 101.3 %all-gather.7.cloned.1.call-start = ((), (), s32[]{:S(2)}) async-start(), calls=%async_computation.1 | async-start | bytes 6684672 | tf_op jit(solution)/shard_map/all_gather | solution.py:65
  9.3 242.8 %all-gather.5.cloned.1.call-start = ((), (), s32[]{:S(2)}) async-start(), calls=%async_computation | async-start | bytes 6684672 | tf_op jit(solution)/shard_map/all_gather | solution.py:50
  10.3 342.1 %all-gather.11.cloned.1.call-start = ((), (), s32[]{:S(2)}) async-start(), calls=%async_computation.3 | async-start | bytes 6684672 | tf_op jit(solution)/shard_map/all_gather | solution.py:65
  21.1 1.1 copy-start.5
  23.0 470.5 %all-gather.9.cloned.1.call-start = ((), (), s32[]{:S(2)}) async-start(), calls=%async_computation.2 | async-start | bytes 6684672 | tf_op jit(solution)/shard_map/all_gather | solution.py:50
  129.0 5.0 copy-start.8
  139.3 112.9 %copy-start.3 = (bf16[2,128,768]{1,2,0:T(8,128)(2,1)S(1)}, bf16[2,128,768]{1,2,0:T(8,128)(2,1)}, u32[]{:S(2)}) copy-start(bf16[2,128,768]{1,2,0:T(8,128)(2,1)} %copy.72) | copy-start | bytes 1179652
  253.0 6.6 %copy-start.7 = (bf16[2,128,384]{1,2,0:T(8,128)(2,1)S(1)}, bf16[2,128,384]{1,2,0:T(8,128)(2,1)}, u32[]{:S(2)}) copy-start(bf16[2,128,384]{1,2,0:T(8,128)(2,1)} %copy.73) | copy-start | bytes 589828
  266.2 6.6 %copy-start.9 = (bf16[2,128,384]{2,1,0:T(8,128)(2,1)S(1)}, bf16[2,128,384]{2,1,0:T(8,128)(2,1)}, u32[]{:S(2)}) copy-start(bf16[2,128,384]{2,1,0:T(8,128)(2,1)} %copy.52) | copy-start | bytes 589828
  272.8 2.8 copy-start.10
  274.5 1.2 copy-start.1
  385.8 3.3 copy-start.4
  494.3 6.7 %copy-start.6 = (bf16[2,128,384]{2,1,0:T(8,128)(2,1)S(1)}, bf16[2,128,384]{2,1,0:T(8,128)(2,1)}, u32[]{:S(2)}) copy-start(bf16[2,128,384]{2,1,0:T(8,128)(2,1)} %get-tuple-element.13) | copy-start | bytes 589828
Sparse Core Ops, SparseCore 0:
  11.3 97.1 all-gather.6
  110.8 141.3 all-gather.4
  255.4 96.9 all-gather.10
  354.0 139.4 all-gather.8
where the time goes:
time: 531 us; the launch traced here: 523 us
  waiting for transfers between devices  349 us (66%)
  local copies, waits for them, and re-layouts  94.2 us (18%)
  matrix products  60.6 us (11%)
  between operations  16 us (3%)
    all_gather x2, waiting for transfers between devices, spatial_attend(): gathered = lax.all_gather(stale, 'patch', axis=1, tiled=True)  210 us
    all_gather x2, waiting for transfers between devices, temporal_attend(): gathered = lax.all_gather(stale, 'frame', axis=0, tiled=True)  139 us
    sub x4, matrix products, softmax_rows(): expo = jnp.exp(scores - top)  23.1 us
    reshape x6, local copies, waits for them, and re-layouts, heads_of(): return block.reshape(block.shape[0], block.shape[1], heads, HEAD_DIM)  21.7 us
    all_gather x2, local copies, waits for them, and re-layouts, temporal_attend(): gathered = lax.all_gather(stale, 'frame', axis=0, tiled=True)  17.2 us
    slice x2, local copies, waits for them, and re-layouts, spatial_attend(): keys = heads_of(keys_all[..., :swidth], SHEADS)  13.3 us
    slice x2, local copies, waits for them, and re-layouts, temporal_attend(): keys_all[..., :twidth]  12.6 us
    unnamed x33, local copies, waits for them, and re-layouts  12 us
  transfers between devices with their start and end apart: 4, of which 4 were waited for; matrix products, arithmetic and copies ran while one was open for 25% of the time, Pallas kernels for 0%

commit v1 on v0

v1 whole, which is shorter than its diff:
```python
import functools
import math

import jax
import jax.numpy as jnp
from jax import lax
from jax.experimental import pallas as pl
from jax.experimental.pallas import tpu as pltpu
from jax.sharding import PartitionSpec as P

MESH = pl.DeviceIdType.MESH
D = 128
SH = 3
TH = 3
WIDTH = 1536
QW = (SH + TH) * D
ROWS = 256
FREQ = 256
STEPS = 2
NEG = -1e30
LOG2 = math.log2(math.e) / math.sqrt(D)
F32 = jnp.float32
BF16 = jnp.bfloat16


def dot_t(a, b):
    return lax.dot_general(a, b, (((1,), (1,)), ((), ())), preferred_element_type=F32)


def iota(shape, dim):
    return lax.broadcasted_iota(jnp.int32, shape, dim)


def split3(value):
    hi = value.astype(BF16).astype(F32)
    mid = (value - hi).astype(BF16).astype(F32)
    return hi, mid, value - hi - mid


def col_to_row(col):
    eye = iota((D, D), 0) == iota((D, D), 1)
    return jnp.sum(jnp.where(eye, col, 0.0), axis=0, keepdims=True)


def sigma_of(index):
    unit = index.astype(F32) / 1000.0
    return 5.0 * unit / (1.0 + 4.0 * unit)


def kernel(
    ts_ref, lat_ref, stale_ref, wqkv_ref, wout_ref, wtime_ref,
    xo_ref, vo_ref, kvo_ref,
    x_v, h_v, vel_v, wqkv_v, wout_v, wtime_v, mods_v,
    qloc, kvloc, kvs, kvt, qs, qt, oss, osr, ots, otr,
    s_v, ol_s, ll_s, ol_t, ll_t, att,
    load_sem, stale_sem, out_sem, kvo_sem,
    ks_s, ks_r, kt_s, kt_r, qs_s, qs_r, qt_s, qt_r, os_s, os_r, ot_s, ot_r,
):
    fi = lax.axis_index("frame")
    pi = lax.axis_index("patch")
    core = lax.rem(fi, 2)
    zh = lax.rem(fi // 2, 2)
    own = (fi // 4) * 2 + core
    half = lax.rem(pi, 4) // 2
    src = (pi // 4) * 2 + lax.rem(pi, 2)
    role = lax.rem(src + 4 * core, 8)

    def patch_at(place, of_half):
        return (place // 2) * 4 + 2 * of_half + lax.rem(place, 2)

    def place_of(pair):
        return lax.rem(pair + 8 - 4 * core, 8)

    def frame_at(owner, group):
        return (owner // 2) * 4 + group * 2 + lax.rem(owner, 2)

    def push(source, target, send, recv, device, is_self):
        @pl.when(is_self)
        def _():
            pltpu.make_async_copy(source, target, recv).start()

        @pl.when(jnp.logical_not(is_self))
        def _():
            pltpu.make_async_remote_copy(
                src_ref=source, dst_ref=target, send_sem=send, recv_sem=recv,
                device_id=device, device_id_type=MESH,
            ).start()

    def take(ref, sem):
        pltpu.make_async_copy(ref, ref, sem).wait()

    def loop(count, body):
        def step(index, carry):
            body(index)
            return carry
        lax.fori_loop(0, count, step, 0)

    def load_stale(block):
        return pltpu.make_async_copy(
            stale_ref.at[:, :, pl.ds(pl.multiple_of(block * D, D), D)],
            kvloc.at[0, block // 3, lax.rem(block, 3)], stale_sem.at[block])

    loop(12, lambda b: load_stale(b).start())
    loads = [
        pltpu.make_async_copy(a, b, load_sem.at[n])
        for n, (a, b) in enumerate(
            [(lat_ref, x_v), (wtime_ref, wtime_v), (wqkv_ref, wqkv_v), (wout_ref, wout_v)])
    ]
    for one in loads:
        one.start()

    barrier = pltpu.get_barrier_semaphore()

    def greet(k):
        pl.semaphore_signal(
            barrier, inc=1, device_id=(fi, lax.rem(pi + k + 1, 16)), device_id_type=MESH)
        pl.semaphore_signal(
            barrier, inc=1, device_id=(lax.rem(fi + k + 1, 16), pi), device_id_type=MESH)

    loop(15, greet)
    loop(12, lambda b: load_stale(b).wait())
    pl.semaphore_wait(barrier, 30)

    def send_kv(k):
        def spatial(n):
            to_half = n // 6
            pair = lax.rem(n, 6)
            frame, head = pair // 3, lax.rem(pair, 3)
            device = patch_at(place_of(pair), to_half)
            slot = src + 8 * jnp.where(to_half == half, 0, 1)
            push(kvloc.at[k, 0:2, head, frame], kvs.at[k, :, slot], ks_s.at[k, n], ks_r.at[k, slot],
                 (fi, device), device == pi)

        def temporal(n):
            group, owner = n // 8, lax.rem(n, 8)
            device = frame_at(owner, group)
            slot = own + 8 * jnp.where(group == zh, 0, 1)
            rows = pl.ds(pl.multiple_of(owner * 16, 16), 16)
            push(kvloc.at[k, 2:4, :, :, rows], kvt.at[k, :, :, slot], kt_s.at[k, n], kt_r.at[k, slot],
                 (device, pi), device == fi)

        loop(12, spatial)
        loop(16, temporal)

    send_kv(0)

    loads[1].wait()
    lane = iota((16, D), 1).astype(F32)
    row = iota((16, D), 0)
    level = jnp.where(
        row < 3, sigma_of(jnp.full((16, D), ts_ref[0], jnp.int32)),
        sigma_of(jnp.full((16, D), ts_ref[1], jnp.int32))) * 1000.0
    angles = level * jnp.exp(-math.log(10000.0) * lane / D)
    part = lax.rem(row, 3)

    def embed(value):
        value = value / (1.0 + jnp.exp(-value))
        hi, mid, low = split3(value)
        return jnp.where(part == 0, hi, jnp.where(part == 1, mid, low)).astype(BF16)

    emb = jnp.concatenate([embed(jnp.cos(angles)), embed(jnp.sin(angles))], axis=1)
    for n in range(0, 3 * WIDTH, 512):
        cols = slice(n, n + 512)
        parts = jnp.dot(emb, wtime_v[:, cols], preferred_element_type=F32)
        for k in range(STEPS):
            mods_v[k : k + 1, cols] = jnp.sum(parts[3 * k : 3 * k + 3], axis=0, keepdims=True)

    loads[0].wait()

    for k in range(STEPS):
        def norm(n):
            rows = pl.ds(pl.multiple_of(n * 32, 32), 32)
            value = x_v[rows, :].astype(F32)
            center = jnp.mean(value, axis=-1, keepdims=True)
            value = value - center
            spread = jnp.mean(value * value, axis=-1, keepdims=True)
            value = value * lax.rsqrt(spread + 1e-06)
            h_v[rows, :] = (
                value * (1.0 + mods_v[k : k + 1, WIDTH : 2 * WIDTH]) + mods_v[k : k + 1, :WIDTH]
            ).astype(BF16)

        loop(ROWS // 32, norm)
        if k == 0:
            loads[2].wait()

        def project(n):
            cols = pl.ds(pl.multiple_of(n * 256, 256), 256)
            return jnp.dot(h_v[...], wqkv_v[:, cols], preferred_element_type=F32).astype(BF16)

        def query(n):
            out = project(n)
            for part_n in range(2):
                qloc[2 * n + part_n] = out[:, part_n * D : (part_n + 1) * D].reshape(2, D, D)

        if k > 0:
            def sent_q(n):
                @pl.when((n < 6) & (n != role))
                def _():
                    take(qs.at[k - 1, 0], qs_s.at[k - 1, n])

                @pl.when(n != own)
                def _():
                    take(qt.at[k - 1, :, 0], qt_s.at[k - 1, n])

            loop(8, sent_q)
        loop(3, query)

        def send_q(pair):
            place = place_of(pair)
            frame, head = pair // 3, lax.rem(pair, 3)
            push(qloc.at[head, frame], qs.at[k, src], qs_s.at[k, pair], qs_r.at[k, src],
                 (fi, patch_at(place, half)), place == src)

        def send_qt(owner):
            rows = pl.ds(pl.multiple_of(owner * 16, 16), 16)
            push(qloc.at[3:6, :, rows], qt.at[k, :, own], qt_s.at[k, owner], qt_r.at[k, own],
                 (frame_at(owner, zh), pi), owner == own)

        loop(6, send_q)
        loop(8, send_qt)

        def fresh(n):
            out = project(n + 3)
            for part_n in range(2):
                block = 2 * n + part_n
                kvloc[k + 1, block // 3, lax.rem(block, 3)] = out[:, part_n * D : (part_n + 1) * D].reshape(2, D, D)

        loop(6, fresh)

        def store_kv(block):
            return pltpu.make_async_copy(
                kvloc.at[STEPS, block // 3, lax.rem(block, 3)],
                kvo_ref.at[:, :, pl.ds(pl.multiple_of(block * D, D), D)], kvo_sem.at[block])

        if k + 1 < STEPS:
            send_kv(k + 1)
        else:
            loop(12, lambda b: store_kv(b).start())

        def local_spatial(pair):
            frame, head = pair // 3, lax.rem(pair, 3)
            scores = dot_t(qloc[head, frame], kvloc[k + 1, 0, head, frame]) * LOG2
            top = jnp.max(scores, axis=-1, keepdims=True)
            expo = jnp.exp2(scores - top)
            total = jnp.sum(expo, axis=-1, keepdims=True)
            out = jnp.dot(expo.astype(BF16), kvloc[k + 1, 1, head, frame], preferred_element_type=F32)
            ol_s[pair] = out / total
            ll_s[pair] = top + jnp.log2(total)

        loop(6, local_spatial)

        def local_temporal(head):
            for frame in range(2):
                q = qloc[3 + head, frame].astype(F32)
                s0, s1 = [
                    jnp.sum(q * kvloc[k + 1, 2, head, f].astype(F32), axis=-1, keepdims=True) * LOG2
                    for f in range(2)
                ]
                top = jnp.maximum(s0, s1)
                e0, e1 = jnp.exp2(s0 - top), jnp.exp2(s1 - top)
                total = e0 + e1
                out = e0 * kvloc[k + 1, 3, head, 0].astype(F32) + e1 * kvloc[k + 1, 3, head, 1].astype(F32)
                ol_t[head, frame] = out / total
                ll_t[head, frame] = top + jnp.log2(total)

        loop(3, local_temporal)

        @pl.when(role < 6)
        def _():
            def arrived(n):
                take(kvs.at[k, :, n], ks_r.at[k, n])

            def arrived_q(n):
                take(qs.at[k, n], qs_r.at[k, n])

            loop(8, arrived_q)
            loop(16, arrived)

            def attend(n):
                q = qs[k, pl.ds(2 * n, 2)].reshape(2 * D, D)
                s_v[...] = dot_t(q, kvs[k, 0].reshape(16 * D, D))
                base = pl.multiple_of(n * 2 * D, 2 * D)
                s_v[0:D, pl.ds(base, D)] = jnp.full((D, D), NEG, F32)
                s_v[D : 2 * D, pl.ds(pl.multiple_of(base + D, D), D)] = jnp.full((D, D), NEG, F32)
                scores = s_v[...]
                top = jnp.max(scores, axis=-1, keepdims=True)
                expo = jnp.exp2((scores - top) * LOG2)
                total = jnp.sum(expo, axis=-1, keepdims=True)
                out = jnp.dot(expo.astype(BF16), kvs[k, 1].reshape(16 * D, D), preferred_element_type=F32)
                out = (out / total).astype(BF16)
                lse = top * LOG2 + jnp.log2(total)
                for part_n in range(2):
                    place = 2 * n + part_n
                    oss[k, place, 0:D] = out[part_n * D : (part_n + 1) * D]
                    hi, mid, low = split3(col_to_row(lse[part_n * D : (part_n + 1) * D]))
                    tile = iota((16, D), 0)
                    oss[k, place, D : D + 16] = jnp.where(
                        tile == 0, hi, jnp.where(tile == 1, mid, jnp.where(tile == 2, low, 0.0))).astype(BF16)
                    push(oss.at[k, place], osr.at[k, role], os_s.at[k, place], os_r.at[k, role],
                         (fi, patch_at(place, half)), place == src)

            loop(4, attend)

        loop(8, lambda n: take(qt.at[k, :, n], qt_r.at[k, n]))
        loop(16, lambda n: take(kvt.at[k, :, :, n], kt_r.at[k, n]))
        rows_i, cols_i = iota((ROWS, 2 * ROWS), 0), iota((ROWS, 2 * ROWS), 1)
        seen = (lax.rem(rows_i, 16) == lax.rem(cols_i, 16)) & (rows_i // 32 != cols_i // 32)
        tile = iota((16, D), 0)
        stats = [jnp.zeros((16, D), F32), jnp.zeros((16, D), F32)]
        for head in range(TH):
            scores = dot_t(qt[k, head].reshape(ROWS, D), kvt[k, 0, head].reshape(2 * ROWS, D))
            scores = jnp.where(seen, scores, NEG)
            top = jnp.max(scores, axis=-1, keepdims=True)
            expo = jnp.exp2((scores - top) * LOG2)
            total = jnp.sum(expo, axis=-1, keepdims=True)
            out = jnp.dot(
                expo.astype(BF16), kvt[k, 1, head].reshape(2 * ROWS, D), preferred_element_type=F32)
            out = (out / total).astype(BF16)
            lse = top * LOG2 + jnp.log2(total)
            ots[k, :, head * 32 : head * 32 + 32] = out.reshape(8, 32, D)
            for chunk in range(2):
                parts = split3(col_to_row(lse[chunk * D : (chunk + 1) * D]))
                for n, value in enumerate(parts):
                    stats[chunk] = jnp.where(tile == 3 * head + n, value, stats[chunk])
        for place in range(8):
            ots[k, place, 96:112] = stats[place // 4].astype(BF16)

        def send_ot(place):
            push(ots.at[k, place], otr.at[k, own], ot_s.at[k, place], ot_r.at[k, own],
                 (frame_at(place, zh), pi), place == own)

        loop(8, send_ot)

        def merge(mine, mine_lse, other, other_lse):
            weight = 1.0 / (1.0 + jnp.exp2(mine_lse - other_lse))
            return (mine + weight * (other.astype(F32) - mine)).astype(BF16)

        for pair in range(6):
            take(osr.at[k, pair], os_r.at[k, pair])
            frame, head = pair // 3, pair % 3
            lse = jnp.sum(osr[k, pair, D : D + 16].astype(F32), axis=0, keepdims=True)
            eye = iota((D, D), 0) == iota((D, D), 1)
            lse = jnp.sum(jnp.where(eye, lse, 0.0), axis=1, keepdims=True)
            att[frame * D : (frame + 1) * D, head * D : (head + 1) * D] = merge(
                ol_s[pair], ll_s[pair], osr[k, pair, 0:D], lse)

        loop(8, lambda n: take(otr.at[k, n], ot_r.at[k, n]))
        pick = iota((32, D), 1) == iota((32, D), 0) + 32 * lax.rem(own, 4)

        def merge_t(owner):
            stat = otr[k, owner, 96:112].astype(F32)
            for head in range(TH):
                lse = jnp.sum(stat[3 * head : 3 * head + 3], axis=0, keepdims=True)
                lse = jnp.sum(jnp.where(pick, lse, 0.0), axis=1, keepdims=True)
                for frame in range(2):
                    rows = pl.ds(pl.multiple_of(owner * 16, 16), 16)
                    att[
                        pl.ds(pl.multiple_of(frame * D + owner * 16, 16), 16),
                        (SH + head) * D : (SH + head + 1) * D,
                    ] = merge(
                        ol_t[head, frame, rows], ll_t[head, frame, rows],
                        otr[k, owner, head * 32 + frame * 16 : head * 32 + frame * 16 + 16],
                        lse[frame * 16 : frame * 16 + 16])

        loop(8, merge_t)

        if k == 0:
            loads[3].wait()
        dsig = (sigma_of(jnp.full((1, 256), ts_ref[k + 1], jnp.int32))
                - sigma_of(jnp.full((1, 256), ts_ref[k], jnp.int32)))

        def stores(n):
            cols = pl.ds(pl.multiple_of(n * 256, 256), 256)
            return [
                pltpu.make_async_copy(x_v.at[:, cols], xo_ref.at[:, cols], out_sem.at[0, n]),
                pltpu.make_async_copy(vel_v.at[:, cols], vo_ref.at[:, cols], out_sem.at[1, n]),
            ]

        def update(n):
            cols = pl.ds(pl.multiple_of(n * 256, 256), 256)
            branch = jnp.dot(att[...], wout_v[:, cols], preferred_element_type=F32)
            vel = mods_v[k : k + 1, pl.ds(pl.multiple_of(2 * WIDTH + n * 256, 256), 256)] * branch
            x_v[:, cols] = (x_v[:, cols].astype(F32) + dsig * vel).astype(BF16)
            if k + 1 == STEPS:
                vel_v[:, cols] = vel.astype(BF16)
                for one in stores(n):
                    one.start()

        loop(WIDTH // 256, update)

    def drained(n):
        for one in stores(n):
            one.wait()

    loop(WIDTH // 256, drained)
    loop(12, lambda b: store_kv(b).wait())
    for k in range(STEPS):
        def sent_ks(n):
            @pl.when(jnp.logical_not((lax.rem(n, 6) == role) & (n // 6 == half)))
            def _():
                take(kvs.at[k, :, 0], ks_s.at[k, n])

        def sent_kt(n):
            @pl.when(n != own + 8 * zh)
            def _():
                take(kvt.at[k, :, :, 0], kt_s.at[k, n])

        def sent_o(n):
            @pl.when((role < 6) & (n != src))
            def _():
                take(oss.at[k, 0], os_s.at[k, n])

            @pl.when(n != own)
            def _():
                take(ots.at[k, 0], ot_s.at[k, n])

        loop(12, sent_ks)
        loop(16, sent_kt)
        loop(8, sent_o)

    def sent_last(n):
        @pl.when((n < 6) & (n != role))
        def _():
            take(qs.at[STEPS - 1, 0], qs_s.at[STEPS - 1, n])

        @pl.when(n != own)
        def _():
            take(qt.at[STEPS - 1, :, 0], qt_s.at[STEPS - 1, n])

    loop(8, sent_last)


def per_device(latent, timesteps, w_qkv, w_out, w_time, stale_kv):
    anywhere = pl.BlockSpec(memory_space=pl.ANY)
    dma = pltpu.SemaphoreType.DMA
    x_out, vel, next_kv = pl.pallas_call(
        kernel,
        out_shape=[
            jax.ShapeDtypeStruct((ROWS, WIDTH), BF16),
            jax.ShapeDtypeStruct((ROWS, WIDTH), BF16),
            jax.ShapeDtypeStruct((2, D, WIDTH), BF16),
        ],
        in_specs=[pl.BlockSpec(memory_space=pltpu.SMEM)] + [anywhere] * 5,
        out_specs=[anywhere] * 3,
        scratch_shapes=[
            pltpu.VMEM((ROWS, WIDTH), BF16),
            pltpu.VMEM((ROWS, WIDTH), BF16),
            pltpu.VMEM((ROWS, WIDTH), BF16),
            pltpu.VMEM((WIDTH, 2304), BF16),
            pltpu.VMEM((QW, WIDTH), BF16),
            pltpu.VMEM((FREQ, 3 * WIDTH), BF16),
            pltpu.VMEM((8, 3 * WIDTH), F32),
            pltpu.VMEM((6, 2, D, D), BF16),
            pltpu.VMEM((3, 4, 3, 2, D, D), BF16),
            pltpu.VMEM((2, 2, 16, D, D), BF16),
            pltpu.VMEM((2, 2, 3, 16, 2, 16, D), BF16),
            pltpu.VMEM((2, 8, D, D), BF16),
            pltpu.VMEM((2, 3, 8, 2, 16, D), BF16),
            pltpu.VMEM((2, 8, D + 16, D), BF16),
            pltpu.VMEM((2, 6, D + 16, D), BF16),
            pltpu.VMEM((2, 8, 112, D), BF16),
            pltpu.VMEM((2, 8, 112, D), BF16),
            pltpu.VMEM((2 * D, 16 * D), F32),
            pltpu.VMEM((6, D, D), F32),
            pltpu.VMEM((6, D, 1), F32),
            pltpu.VMEM((3, 2, D, D), F32),
            pltpu.VMEM((3, 2, D, 1), F32),
            pltpu.VMEM((ROWS, QW), BF16),
            dma((4,)), dma((12,)), dma((2, 6)), dma((12,)),
            dma((2, 12)), dma((2, 16)), dma((2, 16)), dma((2, 16)),
            dma((2, 6)), dma((2, 8)), dma((2, 8)), dma((2, 8)),
            dma((2, 8)), dma((2, 6)), dma((2, 8)), dma((2, 8)),
        ],
        compiler_params=pltpu.CompilerParams(
            collective_id=0, has_side_effects=True, vmem_limit_bytes=50 * 2**20),
        cost_estimate=pl.CostEstimate(
            flops=8_000_000_000, bytes_accessed=18_000_000, transcendentals=5_000_000),
    )(timesteps, latent.reshape(ROWS, WIDTH), stale_kv, w_qkv, w_out, w_time)
    shape = (2, D, WIDTH)
    return x_out.reshape(shape), vel.reshape(shape), next_kv


def solution(mesh):
    tokens = P("frame", "patch", None)
    return jax.shard_map(
        per_device,
        mesh=mesh,
        in_specs=(tokens, P(), P(), P(), P(), tokens),
        out_specs=(tokens, tokens, tokens),
        check_vma=False,
    )
```

time: 531 us -> 116 us (0.22); the launches traced: 523 us -> 115 us
  waiting for transfers between devices: 349 us -> 0 us
  Pallas kernels: 0 us -> 109 us
  local copies, waits for them, and re-layouts: 94.2 us -> 5.55 us
  matrix products: 60.6 us -> 0 us
  between operations: 16 us -> 0.65 us
    all_gather x4 -> x0, waiting for transfers between devices: 349 us -> none  [the longest x2 210 us: spatial_attend(): gathered = lax.all_gather(stale, 'patch', axis=1, tiled=True)]
    pallas_call x0 -> x1, Pallas kernels: none -> 109 us  [per_device(): pl.pallas_call(kernel, out_shape=[jax.ShapeDtypeStruct((ROWS, WIDTH), BF1...]
    dot_general x10 -> x0, matrix products: 37.5 us -> none  [the longest x2 10.3 us: spatial_attend(): jnp.einsum('fhqk,fkhd->fqhd', weights, value_rows, preferred_element_type...]
    slice x11 -> x0, local copies, waits for them, and re-layouts: 33.9 us -> none  [the longest x2 13.3 us: spatial_attend(): keys = heads_of(keys_all[..., :swidth], SHEADS)]
    sub x4 -> x0, matrix products: 23.1 us -> none  [softmax_rows(): expo = jnp.exp(scores - top)]
    reshape x6 -> x0, local copies, waits for them, and re-layouts: 21.7 us -> none  [heads_of(): return block.reshape(block.shape[0], block.shape[1], heads, HEAD_DIM)]
    all_gather x2 -> x0, local copies, waits for them, and re-layouts: 17.2 us -> none  [temporal_attend(): gathered = lax.all_gather(stale, 'frame', axis=0, tiled=True)]
    unnamed x33 -> x9, local copies, waits for them, and re-layouts: 12 us -> 5.55 us
  transfers between devices with their start and end apart: 4 -> 0, of which waited for: 4 -> 0; matrix products, arithmetic and copies ran while one was open for 25% -> 0% of each run, Pallas kernels for 0% -> 0%
where the time goes in v1:
time: 116 us; the launch traced here: 115 us
  Pallas kernels  109 us (94%)
  local copies, waits for them, and re-layouts  5.55 us (5%)
    pallas_call x1, Pallas kernels, per_device(): pl.pallas_call(kernel, out_shape=[jax.ShapeDtypeStruct((ROWS, WIDTH), BF1...  109 us
    unnamed x9, local copies, waits for them, and re-layouts  5.55 us

profile of v1, /device:TPU:1, one launch (start us, length us, event | category | flops | bytes accessed | tf_op | source)
XLA Modules:
  0.0 115.4 jit_solution(6674410955084190389)
XLA Ops:
  0.6 0.0 copy-start
  0.6 1.1 copy-done
  1.8 0.0 copy-start.1
  1.8 1.1 copy-done.1
  2.9 0.0 copy-start.2
  2.9 0.7 copy-done.2
  3.6 109.2 %shard_map.85 = (bf16[256,1536]{1,0:T(8,128)(2,1)S(1)}, bf16[256,1536]{1,0:T(8,128)(2,1)S(1)}, bf16[2,128,1536]{2,1,0:T(8,128)(2,1)S(1)}) custom-call(s32[3]{0:T(128)S(1)} %copy-done.2, bf16[256,1536]{1,0:T(8,128)(2,1)S(1)} %bitcast.5, bf16[2,128,1536]{2,1,0:T(8,128)(2,1)S(1)} %copy-done.1, bf16[1536,2304]{1,0:T(8,128)(2,1)} %wqkv_ref.1, ...), custom_call_target="tpu_custom_call" | custom-call | flops 8000000000 | bytes 18000000 | tf_op jit(solution)/shard_map/pallas_call | solution.py:436
  112.7 0.9 copy.12
  113.6 0.9 copy.13
  114.5 0.9 copy.14
Async XLA Ops:
  0.6 1.1 copy-start
  1.8 1.1 copy-start.1
  2.9 0.7 copy-start.2

commit v2 on v1

--- a/solution.py
+++ b/solution.py
@@ -50,9 +50,9 @@
 def kernel(
     ts_ref, lat_ref, stale_ref, wqkv_ref, wout_ref, wtime_ref,
     xo_ref, vo_ref, kvo_ref,
-    x_v, h_v, vel_v, wqkv_v, wout_v, wtime_v, mods_v,
+    x_v, h_v, vel_v, part_v, wqkv_v, wout_v, wtime_v, mods_v,
     qloc, kvloc, kvs, kvt, qs, qt, oss, osr, ots, otr,
-    s_v, ol_s, ll_s, ol_t, ll_t, att,
+    s_v, p_v, inv_v, ol_s, ll_s, ol_t, ll_t, att,
     load_sem, stale_sem, out_sem, kvo_sem,
     ks_s, ks_r, kt_s, kt_r, qs_s, qs_r, qt_s, qt_r, os_s, os_r, ot_s, ot_r,
 ):
@@ -89,6 +89,15 @@
     def take(ref, sem):
         pltpu.make_async_copy(ref, ref, sem).wait()
 
+    def take_sent(all_of_them, but_one, sem):
+        @pl.when(role < 6)
+        def _():
+            take(but_one, sem)
+
+        @pl.when(role >= 6)
+        def _():
+            take(all_of_them, sem)
+
     def loop(count, body):
         def step(index, carry):
             body(index)
@@ -121,28 +130,32 @@
     loop(12, lambda b: load_stale(b).wait())
     pl.semaphore_wait(barrier, 30)
 
-    def send_kv(k):
-        def spatial(n):
-            to_half = n // 6
+    def send_spatial(k, kv):
+        def one(n):
+            to_half = lax.rem(half + 1 + n // 6, 2)
             pair = lax.rem(n, 6)
             frame, head = pair // 3, lax.rem(pair, 3)
             device = patch_at(place_of(pair), to_half)
             slot = src + 8 * jnp.where(to_half == half, 0, 1)
-            push(kvloc.at[k, 0:2, head, frame], kvs.at[k, :, slot], ks_s.at[k, n], ks_r.at[k, slot],
+            push(kvloc.at[k, kv, head, frame], kvs.at[k, kv, slot], ks_s.at[k, kv], ks_r.at[k, kv],
                  (fi, device), device == pi)
 
-        def temporal(n):
-            group, owner = n // 8, lax.rem(n, 8)
+        loop(12, one)
+
+    def send_temporal(k):
+        def one(n):
+            group = lax.rem(zh + 1 + n // 8, 2)
+            owner = lax.rem(n + own, 8)
             device = frame_at(owner, group)
             slot = own + 8 * jnp.where(group == zh, 0, 1)
             rows = pl.ds(pl.multiple_of(owner * 16, 16), 16)
-            push(kvloc.at[k, 2:4, :, :, rows], kvt.at[k, :, :, slot], kt_s.at[k, n], kt_r.at[k, slot],
+            push(kvloc.at[k, 2:4, :, :, rows], kvt.at[k, :, :, slot], kt_s.at[k], kt_r.at[k],
                  (device, pi), device == fi)
 
-        loop(12, spatial)
-        loop(16, temporal)
-
-    send_kv(0)
+        loop(16, one)
+
+    send_temporal(0)
+    send_spatial(0, 0)
 
     loads[1].wait()
     lane = iota((16, D), 1).astype(F32)
@@ -166,6 +179,10 @@
             mods_v[k : k + 1, cols] = jnp.sum(parts[3 * k : 3 * k + 3], axis=0, keepdims=True)
 
     loads[0].wait()
+
+    def sent_queries(k):
+        take_sent(qs.at[k, 0:6], qs.at[k, 0:5], qs_s.at[k])
+        take(qt.at[k, :, 0:7], qt_s.at[k])
 
     for k in range(STEPS):
         def norm(n):
@@ -193,31 +210,23 @@
                 qloc[2 * n + part_n] = out[:, part_n * D : (part_n + 1) * D].reshape(2, D, D)
 
         if k > 0:
-            def sent_q(n):
-                @pl.when((n < 6) & (n != role))
-                def _():
-                    take(qs.at[k - 1, 0], qs_s.at[k - 1, n])
-
-                @pl.when(n != own)
-                def _():
-                    take(qt.at[k - 1, :, 0], qt_s.at[k - 1, n])
-
-            loop(8, sent_q)
+            sent_queries(k - 1)
         loop(3, query)
 
         def send_q(pair):
             place = place_of(pair)
             frame, head = pair // 3, lax.rem(pair, 3)
-            push(qloc.at[head, frame], qs.at[k, src], qs_s.at[k, pair], qs_r.at[k, src],
+            push(qloc.at[head, frame], qs.at[k, src], qs_s.at[k], qs_r.at[k],
                  (fi, patch_at(place, half)), place == src)
 
         def send_qt(owner):
             rows = pl.ds(pl.multiple_of(owner * 16, 16), 16)
-            push(qloc.at[3:6, :, rows], qt.at[k, :, own], qt_s.at[k, owner], qt_r.at[k, own],
+            push(qloc.at[3:6, :, rows], qt.at[k, :, own], qt_s.at[k], qt_r.at[k],
                  (frame_at(owner, zh), pi), owner == own)
 
         loop(6, send_q)
         loop(8, send_qt)
+        send_spatial(k, 1)
 
         def fresh(n):
             out = project(n + 3)
@@ -232,13 +241,11 @@
                 kvloc.at[STEPS, block // 3, lax.rem(block, 3)],
                 kvo_ref.at[:, :, pl.ds(pl.multiple_of(block * D, D), D)], kvo_sem.at[block])
 
-        if k + 1 < STEPS:
-            send_kv(k + 1)
-        else:
+        if k + 1 == STEPS:
             loop(12, lambda b: store_kv(b).start())
 
         def local_spatial(pair):
-            frame, head = pair // 3, lax.rem(pair, 3)
+            frame, head = pair // 3, pair % 3
             scores = dot_t(qloc[head, frame], kvloc[k + 1, 0, head, frame]) * LOG2
             top = jnp.max(scores, axis=-1, keepdims=True)
             expo = jnp.exp2(scores - top)
@@ -247,7 +254,8 @@
             ol_s[pair] = out / total
             ll_s[pair] = top + jnp.log2(total)
 
-        loop(6, local_spatial)
+        for pair in range(6):
+            local_spatial(pair)
 
         def local_temporal(head):
             for frame in range(2):
@@ -263,46 +271,11 @@
                 ol_t[head, frame] = out / total
                 ll_t[head, frame] = top + jnp.log2(total)
 
-        loop(3, local_temporal)
-
-        @pl.when(role < 6)
-        def _():
-            def arrived(n):
-                take(kvs.at[k, :, n], ks_r.at[k, n])
-
-            def arrived_q(n):
-                take(qs.at[k, n], qs_r.at[k, n])
-
-            loop(8, arrived_q)
-            loop(16, arrived)
-
-            def attend(n):
-                q = qs[k, pl.ds(2 * n, 2)].reshape(2 * D, D)
-                s_v[...] = dot_t(q, kvs[k, 0].reshape(16 * D, D))
-                base = pl.multiple_of(n * 2 * D, 2 * D)
-                s_v[0:D, pl.ds(base, D)] = jnp.full((D, D), NEG, F32)
-                s_v[D : 2 * D, pl.ds(pl.multiple_of(base + D, D), D)] = jnp.full((D, D), NEG, F32)
-                scores = s_v[...]
-                top = jnp.max(scores, axis=-1, keepdims=True)
-                expo = jnp.exp2((scores - top) * LOG2)
-                total = jnp.sum(expo, axis=-1, keepdims=True)
-                out = jnp.dot(expo.astype(BF16), kvs[k, 1].reshape(16 * D, D), preferred_element_type=F32)
-                out = (out / total).astype(BF16)
-                lse = top * LOG2 + jnp.log2(total)
-                for part_n in range(2):
-                    place = 2 * n + part_n
-                    oss[k, place, 0:D] = out[part_n * D : (part_n + 1) * D]
-                    hi, mid, low = split3(col_to_row(lse[part_n * D : (part_n + 1) * D]))
-                    tile = iota((16, D), 0)
-                    oss[k, place, D : D + 16] = jnp.where(
-                        tile == 0, hi, jnp.where(tile == 1, mid, jnp.where(tile == 2, low, 0.0))).astype(BF16)
-                    push(oss.at[k, place], osr.at[k, role], os_s.at[k, place], os_r.at[k, role],
-                         (fi, patch_at(place, half)), place == src)
-
-            loop(4, attend)
-
-        loop(8, lambda n: take(qt.at[k, :, n], qt_r.at[k, n]))
-        loop(16, lambda n: take(kvt.at[k, :, :, n], kt_r.at[k, n]))
+        for head in range(TH):
+            local_temporal(head)
+
+        take(qt.at[k], qt_r.at[k])
+        take(kvt.at[k], kt_r.at[k])
         rows_i, cols_i = iota((ROWS, 2 * ROWS), 0), iota((ROWS, 2 * ROWS), 1)
         seen = (lax.rem(rows_i, 16) == lax.rem(cols_i, 16)) & (rows_i // 32 != cols_i // 32)
         tile = iota((16, D), 0)
@@ -326,46 +299,102 @@
             ots[k, place, 96:112] = stats[place // 4].astype(BF16)
 
         def send_ot(place):
-            push(ots.at[k, place], otr.at[k, own], ot_s.at[k, place], ot_r.at[k, own],
+            push(ots.at[k, place], otr.at[k, own], ot_s.at[k], ot_r.at[k],
                  (frame_at(place, zh), pi), place == own)
 
         loop(8, send_ot)
+        if k + 1 < STEPS:
+            send_spatial(k + 1, 0)
+
+        @pl.when(role < 6)
+        def _():
+            take(qs.at[k], qs_r.at[k])
+            take(kvs.at[k, 0], ks_r.at[k, 0])
+
+            def weigh(n):
+                q = qs[k, pl.ds(2 * n, 2)].reshape(2 * D, D)
+                s_v[...] = dot_t(q, kvs[k, 0].reshape(16 * D, D))
+                base = pl.multiple_of(n * 2 * D, 2 * D)
+                s_v[0:D, pl.ds(base, D)] = jnp.full((D, D), NEG, F32)
+                s_v[D : 2 * D, pl.ds(pl.multiple_of(base + D, D), D)] = jnp.full((D, D), NEG, F32)
+                scores = s_v[...]
+                top = jnp.max(scores, axis=-1, keepdims=True)
+                expo = jnp.exp2((scores - top) * LOG2)
+                total = jnp.sum(expo, axis=-1, keepdims=True)
+                p_v[pl.ds(base, 2 * D), :] = expo.astype(BF16)
+                inv_v[pl.ds(base, 2 * D), :] = 1.0 / total
+                lse = top * LOG2 + jnp.log2(total)
+                for part_n in range(2):
+                    hi, mid, low = split3(col_to_row(lse[part_n * D : (part_n + 1) * D]))
+                    tile = iota((16, D), 0)
+                    oss[k, 2 * n + part_n, D : D + 16] = jnp.where(
+                        tile == 0, hi, jnp.where(tile == 1, mid, jnp.where(tile == 2, low, 0.0))).astype(BF16)
+
+            loop(4, weigh)
 
         def merge(mine, mine_lse, other, other_lse):
             weight = 1.0 / (1.0 + jnp.exp2(mine_lse - other_lse))
             return (mine + weight * (other.astype(F32) - mine)).astype(BF16)
 
+        def columns(pick, stat, at):
+            lse = dot_t(pick.astype(BF16), stat)
+            return [jnp.sum(lse[:, c : c + 3], axis=-1, keepdims=True) for c in at]
+
+        def finish_temporal():
+            take(otr.at[k], ot_r.at[k])
+            pick = iota((32, D), 1) == iota((32, D), 0) + 32 * lax.rem(own, 4)
+            lse_t = columns(
+                pick, otr[k, :, 96:112].reshape(8 * 16, D), [16 * o + 3 * h for o in range(8) for h in range(TH)])
+            for owner in range(8):
+                for head in range(TH):
+                    for frame in range(2):
+                        rows = slice(owner * 16, owner * 16 + 16)
+                        att[frame * D + owner * 16 : frame * D + owner * 16 + 16, (SH + head) * D : (SH + head + 1) * D] = merge(
+                            ol_t[head, frame, rows], ll_t[head, frame, rows],
+                            otr[k, owner, head * 32 + frame * 16 : head * 32 + frame * 16 + 16],
+                            lse_t[owner * TH + head][frame * 16 : frame * 16 + 16])
+            if k == 0:
+                loads[3].wait()
+
+            def first_half(n):
+                cols = pl.ds(pl.multiple_of(n * 256, 256), 256)
+                part_v[:, cols] = jnp.dot(
+                    att[:, SH * D :], wout_v[SH * D :, cols], preferred_element_type=F32)
+
+            loop(WIDTH // 256, first_half)
+
+        if k + 1 == STEPS:
+            finish_temporal()
+
+        @pl.when(role < 6)
+        def _():
+            take(kvs.at[k, 1], ks_r.at[k, 1])
+
+            def attend(turn):
+                n = lax.rem(turn + role, 4)
+                rows = pl.ds(pl.multiple_of(n * 2 * D, 2 * D), 2 * D)
+                out = jnp.dot(p_v[rows, :], kvs[k, 1].reshape(16 * D, D), preferred_element_type=F32)
+                out = (out * inv_v[rows, :]).astype(BF16)
+                for part_n in range(2):
+                    place = 2 * n + part_n
+                    oss[k, place, 0:D] = out[part_n * D : (part_n + 1) * D]
+                    push(oss.at[k, place], osr.at[k, role], os_s.at[k], os_r.at[k],
+                         (fi, patch_at(place, half)), place == src)
+
+            loop(4, attend)
+
+        if k + 1 < STEPS:
+            send_temporal(k + 1)
+            finish_temporal()
+
+        take(osr.at[k], os_r.at[k])
+        lse_s = columns(
+            iota((D, D), 0) == iota((D, D), 1), osr[k, :, D : D + 16].reshape(6 * 16, D), [16 * p for p in range(6)])
         for pair in range(6):
-            take(osr.at[k, pair], os_r.at[k, pair])
             frame, head = pair // 3, pair % 3
-            lse = jnp.sum(osr[k, pair, D : D + 16].astype(F32), axis=0, keepdims=True)
-            eye = iota((D, D), 0) == iota((D, D), 1)
-            lse = jnp.sum(jnp.where(eye, lse, 0.0), axis=1, keepdims=True)
             att[frame * D : (frame + 1) * D, head * D : (head + 1) * D] = merge(
-                ol_s[pair], ll_s[pair], osr[k, pair, 0:D], lse)
-
-        loop(8, lambda n: take(otr.at[k, n], ot_r.at[k, n]))
-        pick = iota((32, D), 1) == iota((32, D), 0) + 32 * lax.rem(own, 4)
-
-        def merge_t(owner):
-            stat = otr[k, owner, 96:112].astype(F32)
-            for head in range(TH):
-                lse = jnp.sum(stat[3 * head : 3 * head + 3], axis=0, keepdims=True)
-                lse = jnp.sum(jnp.where(pick, lse, 0.0), axis=1, keepdims=True)
-                for frame in range(2):
-                    rows = pl.ds(pl.multiple_of(owner * 16, 16), 16)
-                    att[
-                        pl.ds(pl.multiple_of(frame * D + owner * 16, 16), 16),
-                        (SH + head) * D : (SH + head + 1) * D,
-                    ] = merge(
-                        ol_t[head, frame, rows], ll_t[head, frame, rows],
-                        otr[k, owner, head * 32 + frame * 16 : head * 32 + frame * 16 + 16],
-                        lse[frame * 16 : frame * 16 + 16])
-
-        loop(8, merge_t)
-
-        if k == 0:
-            loads[3].wait()
+                ol_s[pair], ll_s[pair], osr[k, pair, 0:D], lse_s[pair])
+
         dsig = (sigma_of(jnp.full((1, 256), ts_ref[k + 1], jnp.int32))
                 - sigma_of(jnp.full((1, 256), ts_ref[k], jnp.int32)))
 
@@ -378,7 +407,8 @@
 
         def update(n):
             cols = pl.ds(pl.multiple_of(n * 256, 256), 256)
-            branch = jnp.dot(att[...], wout_v[:, cols], preferred_element_type=F32)
+            branch = part_v[:, cols] + jnp.dot(
+                att[:, : SH * D], wout_v[: SH * D, cols], preferred_element_type=F32)
             vel = mods_v[k : k + 1, pl.ds(pl.multiple_of(2 * WIDTH + n * 256, 256), 256)] * branch
             x_v[:, cols] = (x_v[:, cols].astype(F32) + dsig * vel).astype(BF16)
             if k + 1 == STEPS:
@@ -388,64 +418,58 @@
 
         loop(WIDTH // 256, update)
 
-    def drained(n):
+    for k in range(STEPS):
+        for kv in range(2):
+            take_sent(kvs.at[k, kv, 0:12], kvs.at[k, kv, 0:11], ks_s.at[k, kv])
+        take(kvt.at[k, :, :, 0:15], kt_s.at[k])
+
+        @pl.when(role < 6)
+        def _():
+            take(oss.at[k, 0:7], os_s.at[k])
+
+        take(ots.at[k, 0:7], ot_s.at[k])
+    sent_queries(STEPS - 1)
+    loop(12, lambda b: store_kv(b).wait())
+
+    def stored(n):
         for one in stores(n):
             one.wait()
 
-    loop(WIDTH // 256, drained)
-    loop(12, lambda b: store_kv(b).wait())
-    for k in range(STEPS):
-        def sent_ks(n):
-            @pl.when(jnp.logical_not((lax.rem(n, 6) == role) & (n // 6 == half)))
-            def _():
-                take(kvs.at[k, :, 0], ks_s.at[k, n])
-
-        def sent_kt(n):
-            @pl.when(n != own + 8 * zh)
-            def _():
-                take(kvt.at[k, :, :, 0], kt_s.at[k, n])
-
-        def sent_o(n):
-            @pl.when((role < 6) & (n != src))
-            def _():
-                take(oss.at[k, 0], os_s.at[k, n])
-
-            @pl.when(n != own)
-            def _():
-                take(ots.at[k, 0], ot_s.at[k, n])
-
-        loop(12, sent_ks)
-        loop(16, sent_kt)
-        loop(8, sent_o)
-
-    def sent_last(n):
-        @pl.when((n < 6) & (n != role))
-        def _():
-            take(qs.at[STEPS - 1, 0], qs_s.at[STEPS - 1, n])
-
-        @pl.when(n != own)
-        def _():
-            take(qt.at[STEPS - 1, :, 0], qt_s.at[STEPS - 1, n])
-
-    loop(8, sent_last)
+    loop(WIDTH // 256, stored)
+
+
+def hand_on(a_ref, b_ref, c_ref, ao_ref, bo_ref, co_ref, a_v, b_v, c_v, in_sem, out_sem):
+    moves = [
+        (pltpu.make_async_copy(a, v, in_sem.at[n]), pltpu.make_async_copy(v, b, out_sem.at[n]))
+        for n, (a, v, b) in enumerate([(a_ref, a_v, ao_ref), (b_ref, b_v, bo_ref), (c_ref, c_v, co_ref)])
+    ]
+    for into, _ in moves:
+        into.start()
+    for into, out in moves:
+        into.wait()
+        out.start()
+    for _, out in moves:
+        out.wait()
 
 
 def per_device(latent, timesteps, w_qkv, w_out, w_time, stale_kv):
     anywhere = pl.BlockSpec(memory_space=pl.ANY)
     dma = pltpu.SemaphoreType.DMA
-    x_out, vel, next_kv = pl.pallas_call(
+    results = [
+        jax.ShapeDtypeStruct((ROWS, WIDTH), BF16),
+        jax.ShapeDtypeStruct((ROWS, WIDTH), BF16),
+        jax.ShapeDtypeStruct((2, D, WIDTH), BF16),
+    ]
+    made = pl.pallas_call(
         kernel,
-        out_shape=[
-            jax.ShapeDtypeStruct((ROWS, WIDTH), BF16),
-            jax.ShapeDtypeStruct((ROWS, WIDTH), BF16),
-            jax.ShapeDtypeStruct((2, D, WIDTH), BF16),
-        ],
+        out_shape=results,
         in_specs=[pl.BlockSpec(memory_space=pltpu.SMEM)] + [anywhere] * 5,
         out_specs=[anywhere] * 3,
         scratch_shapes=[
             pltpu.VMEM((ROWS, WIDTH), BF16),
             pltpu.VMEM((ROWS, WIDTH), BF16),
             pltpu.VMEM((ROWS, WIDTH), BF16),
+            pltpu.VMEM((ROWS, WIDTH), F32),
             pltpu.VMEM((WIDTH, 2304), BF16),
             pltpu.VMEM((QW, WIDTH), BF16),
             pltpu.VMEM((FREQ, 3 * WIDTH), BF16),
@@ -461,21 +485,31 @@
             pltpu.VMEM((2, 8, 112, D), BF16),
             pltpu.VMEM((2, 8, 112, D), BF16),
             pltpu.VMEM((2 * D, 16 * D), F32),
+            pltpu.VMEM((8 * D, 16 * D), BF16),
+            pltpu.VMEM((8 * D, 1), F32),
             pltpu.VMEM((6, D, D), F32),
             pltpu.VMEM((6, D, 1), F32),
             pltpu.VMEM((3, 2, D, D), F32),
             pltpu.VMEM((3, 2, D, 1), F32),
             pltpu.VMEM((ROWS, QW), BF16),
             dma((4,)), dma((12,)), dma((2, 6)), dma((12,)),
-            dma((2, 12)), dma((2, 16)), dma((2, 16)), dma((2, 16)),
-            dma((2, 6)), dma((2, 8)), dma((2, 8)), dma((2, 8)),
-            dma((2, 8)), dma((2, 6)), dma((2, 8)), dma((2, 8)),
+            dma((2, 2)), dma((2, 2)), dma((2,)), dma((2,)),
+            dma((2,)), dma((2,)), dma((2,)), dma((2,)),
+            dma((2,)), dma((2,)), dma((2,)), dma((2,)),
         ],
         compiler_params=pltpu.CompilerParams(
-            collective_id=0, has_side_effects=True, vmem_limit_bytes=50 * 2**20),
+            collective_id=0, has_side_effects=True, vmem_limit_bytes=62 * 2**20),
         cost_estimate=pl.CostEstimate(
             flops=8_000_000_000, bytes_accessed=18_000_000, transcendentals=5_000_000),
     )(timesteps, latent.reshape(ROWS, WIDTH), stale_kv, w_qkv, w_out, w_time)
+    x_out, vel, next_kv = pl.pallas_call(
+        hand_on,
+        out_shape=results,
+        in_specs=[anywhere] * 3,
+        out_specs=[anywhere] * 3,
+        scratch_shapes=[pltpu.VMEM(one.shape, BF16) for one in results] + [dma((3,)), dma((3,))],
+        compiler_params=pltpu.CompilerParams(vmem_limit_bytes=60 * 2**20),
+    )(*made)
     shape = (2, D, WIDTH)
     return x_out.reshape(shape), vel.reshape(shape), next_kv
 

time: 116 us -> 103 us (0.89)
  Pallas kernels: 109 us -> 102 us
  local copies, waits for them, and re-layouts: 5.55 us -> 0 us
    pallas_call x1 -> x2, Pallas kernels: 109 us -> 102 us  [the longest x1 99.5 us: per_device(): pl.pallas_call(kernel, out_shape=results, in_specs=[pl.BlockSpec(memory_s...]
    unnamed x9 -> x0, local copies, waits for them, and re-layouts: 5.55 us -> none
where the time goes in v2:
time: 103 us
  Pallas kernels  102 us (99%)
    pallas_call x1, Pallas kernels, per_device(): pl.pallas_call(kernel, out_shape=results, in_specs=[pl.BlockSpec(memory_s...  99.5 us
    pallas_call x1, Pallas kernels, per_device(): pl.pallas_call(hand_on, out_shape=results, in_specs=[anywhere] * 3, out_s...  2.58 us

profile of v2, /device:TPU:1, one launch (start us, length us, event | category | flops | bytes accessed | tf_op | source)
XLA Modules:
  0.0 102.7 jit_solution(12892976790703909535)
XLA Ops:
  0.6 99.5 %shard_map.85 = (bf16[256,1536]{1,0:T(8,128)(2,1)}, bf16[256,1536]{1,0:T(8,128)(2,1)}, bf16[2,128,1536]{2,1,0:T(8,128)(2,1)}) custom-call(s32[3]{0:T(128)} %ts_ref.1, bf16[256,1536]{1,0:T(8,128)(2,1)} %bitcast.3, bf16[2,128,1536]{2,1,0:T(8,128)(2,1)} %stale_ref.1, bf16[1536,2304]{1,0:T(8,128)(2,1)} %wqkv_ref.1, bf16[768,1536]{1,0:T(8,128)(2,1)} %wout_ref.1, ...), custom_call_target="tpu_custom_call" | custom-call | flops 8000000000 | bytes 18000000 | tf_op jit(solution)/shard_map/pallas_call | solution.py:463
  100.2 2.6 %shard_map.86 = (bf16[256,1536]{1,0:T(8,128)(2,1)}, bf16[256,1536]{1,0:T(8,128)(2,1)}, bf16[2,128,1536]{2,1,0:T(8,128)(2,1)}) custom-call(bf16[256,1536]{1,0:T(8,128)(2,1)} %get-tuple-element.9.a_ref, bf16[256,1536]{1,0:T(8,128)(2,1)} %get-tuple-element.10.b_ref, bf16[2,128,1536]{2,1,0:T(8,128)(2,1)} %get-tuple-element.11.c_ref), custom_call_target="tpu_custom_call" | custom-call | tf_op jit(solution)/shard_map/pallas_call | solution.py:505

commit v3 on v2

--- a/solution.py
+++ b/solution.py
@@ -104,6 +104,16 @@
             return carry
         lax.fori_loop(0, count, step, 0)
 
+    barrier = pltpu.get_barrier_semaphore()
+
+    def greet(k):
+        pl.semaphore_signal(
+            barrier, inc=1, device_id=(fi, lax.rem(pi + k + 1, 16)), device_id_type=MESH)
+        pl.semaphore_signal(
+            barrier, inc=1, device_id=(lax.rem(fi + k + 1, 16), pi), device_id_type=MESH)
+
+    loop(15, greet)
+
     def load_stale(block):
         return pltpu.make_async_copy(
             stale_ref.at[:, :, pl.ds(pl.multiple_of(block * D, D), D)],
@@ -118,15 +128,6 @@
     for one in loads:
         one.start()
 
-    barrier = pltpu.get_barrier_semaphore()
-
-    def greet(k):
-        pl.semaphore_signal(
-            barrier, inc=1, device_id=(fi, lax.rem(pi + k + 1, 16)), device_id_type=MESH)
-        pl.semaphore_signal(
-            barrier, inc=1, device_id=(lax.rem(fi + k + 1, 16), pi), device_id_type=MESH)
-
-    loop(15, greet)
     loop(12, lambda b: load_stale(b).wait())
     pl.semaphore_wait(barrier, 30)
 
@@ -142,19 +143,19 @@
 
         loop(12, one)
 
-    def send_temporal(k):
-        def one(n):
-            group = lax.rem(zh + 1 + n // 8, 2)
-            owner = lax.rem(n + own, 8)
+    def send_temporal(k, first, count):
+        def one(turn):
+            n = first + turn
+            group = lax.rem(zh + 1 + n, 2)
+            owner = lax.rem(n // 2 + own, 8)
             device = frame_at(owner, group)
             slot = own + 8 * jnp.where(group == zh, 0, 1)
             rows = pl.ds(pl.multiple_of(owner * 16, 16), 16)
             push(kvloc.at[k, 2:4, :, :, rows], kvt.at[k, :, :, slot], kt_s.at[k], kt_r.at[k],
                  (device, pi), device == fi)
 
-        loop(16, one)
-
-    send_temporal(0)
+        loop(count, one)
+
     send_spatial(0, 0)
 
     loads[1].wait()
@@ -226,7 +227,11 @@
 
         loop(6, send_q)
         loop(8, send_qt)
-        send_spatial(k, 1)
+        if k == 0:
+            send_spatial(0, 1)
+            send_temporal(0, 0, 16)
+        else:
+            send_temporal(1, 8, 8)
 
         def fresh(n):
             out = project(n + 3)
@@ -273,6 +278,53 @@
 
         for head in range(TH):
             local_temporal(head)
+
+        @pl.when(role < 6)
+        def _():
+            take(qs.at[k], qs_r.at[k])
+            take(kvs.at[k, 0], ks_r.at[k, 0])
+
+            def weigh(n):
+                q = qs[k, pl.ds(2 * n, 2)].reshape(2 * D, D)
+                s_v[...] = dot_t(q, kvs[k, 0].reshape(16 * D, D))
+                base = pl.multiple_of(n * 2 * D, 2 * D)
+                s_v[0:D, pl.ds(base, D)] = jnp.full((D, D), NEG, F32)
+                s_v[D : 2 * D, pl.ds(pl.multiple_of(base + D, D), D)] = jnp.full((D, D), NEG, F32)
+                scores = s_v[...]
+                top = jnp.max(scores, axis=-1, keepdims=True)
+                expo = jnp.exp2((scores - top) * LOG2)
+                total = jnp.sum(expo, axis=-1, keepdims=True)
+                p_v[pl.ds(base, 2 * D), :] = expo.astype(BF16)
+                inv_v[pl.ds(base, 2 * D), :] = 1.0 / total
+                lse = top * LOG2 + jnp.log2(total)
+                for part_n in range(2):
+                    hi, mid, low = split3(col_to_row(lse[part_n * D : (part_n + 1) * D]))
+                    tile = iota((16, D), 0)
+                    oss[k, 2 * n + part_n, D : D + 16] = jnp.where(
+                        tile == 0, hi, jnp.where(tile == 1, mid, jnp.where(tile == 2, low, 0.0))).astype(BF16)
+
+            loop(4, weigh)
+
+        @pl.when(role < 6)
+        def _():
+            take(kvs.at[k, 1], ks_r.at[k, 1])
+
+            def attend(turn):
+                n = lax.rem(turn + role, 4)
+                rows = pl.ds(pl.multiple_of(n * 2 * D, 2 * D), 2 * D)
+                out = jnp.dot(p_v[rows, :], kvs[k, 1].reshape(16 * D, D), preferred_element_type=F32)
+                out = (out * inv_v[rows, :]).astype(BF16)
+                for part_n in range(2):
+                    place = 2 * n + part_n
+                    oss[k, place, 0:D] = out[part_n * D : (part_n + 1) * D]
+                    push(oss.at[k, place], osr.at[k, role], os_s.at[k], os_r.at[k],
+                         (fi, patch_at(place, half)), place == src)
+
+            loop(4, attend)
+
+        if k + 1 < STEPS:
+            send_spatial(1, 0)
+            send_spatial(1, 1)
 
         take(qt.at[k], qt_r.at[k])
         take(kvt.at[k], kt_r.at[k])
@@ -303,34 +355,9 @@
                  (frame_at(place, zh), pi), place == own)
 
         loop(8, send_ot)
+
         if k + 1 < STEPS:
-            send_spatial(k + 1, 0)
-
-        @pl.when(role < 6)
-        def _():
-            take(qs.at[k], qs_r.at[k])
-            take(kvs.at[k, 0], ks_r.at[k, 0])
-
-            def weigh(n):
-                q = qs[k, pl.ds(2 * n, 2)].reshape(2 * D, D)
-                s_v[...] = dot_t(q, kvs[k, 0].reshape(16 * D, D))
-                base = pl.multiple_of(n * 2 * D, 2 * D)
-                s_v[0:D, pl.ds(base, D)] = jnp.full((D, D), NEG, F32)
-                s_v[D : 2 * D, pl.ds(pl.multiple_of(base + D, D), D)] = jnp.full((D, D), NEG, F32)
-                scores = s_v[...]
-                top = jnp.max(scores, axis=-1, keepdims=True)
-                expo = jnp.exp2((scores - top) * LOG2)
-                total = jnp.sum(expo, axis=-1, keepdims=True)
-                p_v[pl.ds(base, 2 * D), :] = expo.astype(BF16)
-                inv_v[pl.ds(base, 2 * D), :] = 1.0 / total
-                lse = top * LOG2 + jnp.log2(total)
-                for part_n in range(2):
-                    hi, mid, low = split3(col_to_row(lse[part_n * D : (part_n + 1) * D]))
-                    tile = iota((16, D), 0)
-                    oss[k, 2 * n + part_n, D : D + 16] = jnp.where(
-                        tile == 0, hi, jnp.where(tile == 1, mid, jnp.where(tile == 2, low, 0.0))).astype(BF16)
-
-            loop(4, weigh)
+            send_temporal(1, 0, 8)
 
         def merge(mine, mine_lse, other, other_lse):
             weight = 1.0 / (1.0 + jnp.exp2(mine_lse - other_lse))
@@ -339,53 +366,6 @@
         def columns(pick, stat, at):
             lse = dot_t(pick.astype(BF16), stat)
             return [jnp.sum(lse[:, c : c + 3], axis=-1, keepdims=True) for c in at]
-
-        def finish_temporal():
-            take(otr.at[k], ot_r.at[k])
-            pick = iota((32, D), 1) == iota((32, D), 0) + 32 * lax.rem(own, 4)
-            lse_t = columns(
-                pick, otr[k, :, 96:112].reshape(8 * 16, D), [16 * o + 3 * h for o in range(8) for h in range(TH)])
-            for owner in range(8):
-                for head in range(TH):
-                    for frame in range(2):
-                        rows = slice(owner * 16, owner * 16 + 16)
-                        att[frame * D + owner * 16 : frame * D + owner * 16 + 16, (SH + head) * D : (SH + head + 1) * D] = merge(
-                            ol_t[head, frame, rows], ll_t[head, frame, rows],
-                            otr[k, owner, head * 32 + frame * 16 : head * 32 + frame * 16 + 16],
-                            lse_t[owner * TH + head][frame * 16 : frame * 16 + 16])
-            if k == 0:
-                loads[3].wait()
-
-            def first_half(n):
-                cols = pl.ds(pl.multiple_of(n * 256, 256), 256)
-                part_v[:, cols] = jnp.dot(
-                    att[:, SH * D :], wout_v[SH * D :, cols], preferred_element_type=F32)
-
-            loop(WIDTH // 256, first_half)
-
-        if k + 1 == STEPS:
-            finish_temporal()
-
-        @pl.when(role < 6)
-        def _():
-            take(kvs.at[k, 1], ks_r.at[k, 1])
-
-            def attend(turn):
-                n = lax.rem(turn + role, 4)
-                rows = pl.ds(pl.multiple_of(n * 2 * D, 2 * D), 2 * D)
-                out = jnp.dot(p_v[rows, :], kvs[k, 1].reshape(16 * D, D), preferred_element_type=F32)
-                out = (out * inv_v[rows, :]).astype(BF16)
-                for part_n in range(2):
-                    place = 2 * n + part_n
-                    oss[k, place, 0:D] = out[part_n * D : (part_n + 1) * D]
-                    push(oss.at[k, place], osr.at[k, role], os_s.at[k], os_r.at[k],
-                         (fi, patch_at(place, half)), place == src)
-
-            loop(4, attend)
-
-        if k + 1 < STEPS:
-            send_temporal(k + 1)
-            finish_temporal()
 
         take(osr.at[k], os_r.at[k])
         lse_s = columns(
@@ -395,6 +375,29 @@
             att[frame * D : (frame + 1) * D, head * D : (head + 1) * D] = merge(
                 ol_s[pair], ll_s[pair], osr[k, pair, 0:D], lse_s[pair])
 
+        if k == 0:
+            loads[3].wait()
+
+        def first_half(n):
+            cols = pl.ds(pl.multiple_of(n * 256, 256), 256)
+            part_v[:, cols] = jnp.dot(
+                att[:, : SH * D], wout_v[: SH * D, cols], preferred_element_type=F32)
+
+        loop(WIDTH // 256, first_half)
+
+        take(otr.at[k], ot_r.at[k])
+        pick = iota((32, D), 1) == iota((32, D), 0) + 32 * lax.rem(own, 4)
+        lse_t = columns(
+            pick, otr[k, :, 96:112].reshape(8 * 16, D), [16 * o + 3 * h for o in range(8) for h in range(TH)])
+        for owner in range(8):
+            for head in range(TH):
+                for frame in range(2):
+                    rows = slice(owner * 16, owner * 16 + 16)
+                    att[frame * D + owner * 16 : frame * D + owner * 16 + 16, (SH + head) * D : (SH + head + 1) * D] = merge(
+                        ol_t[head, frame, rows], ll_t[head, frame, rows],
+                        otr[k, owner, head * 32 + frame * 16 : head * 32 + frame * 16 + 16],
+                        lse_t[owner * TH + head][frame * 16 : frame * 16 + 16])
+
         dsig = (sigma_of(jnp.full((1, 256), ts_ref[k + 1], jnp.int32))
                 - sigma_of(jnp.full((1, 256), ts_ref[k], jnp.int32)))
 
@@ -408,7 +411,7 @@
         def update(n):
             cols = pl.ds(pl.multiple_of(n * 256, 256), 256)
             branch = part_v[:, cols] + jnp.dot(
-                att[:, : SH * D], wout_v[: SH * D, cols], preferred_element_type=F32)
+                att[:, SH * D :], wout_v[SH * D :, cols], preferred_element_type=F32)
             vel = mods_v[k : k + 1, pl.ds(pl.multiple_of(2 * WIDTH + n * 256, 256), 256)] * branch
             x_v[:, cols] = (x_v[:, cols].astype(F32) + dsig * vel).astype(BF16)
             if k + 1 == STEPS:

time: 103 us -> 97.4 us (0.946)
  Pallas kernels: 102 us -> 96.5 us
    pallas_call x1, Pallas kernels: 99.5 us -> 93.9 us  [per_device(): pl.pallas_call(kernel, out_shape=results, in_specs=[pl.BlockSpec(memory_s...]
where the time goes in v3:
time: 97.4 us; the launch traced here: 97.1 us
  Pallas kernels  96.5 us (99%)
    pallas_call x1, Pallas kernels, per_device(): pl.pallas_call(kernel, out_shape=results, in_specs=[pl.BlockSpec(memory_s...  93.9 us
    pallas_call x1, Pallas kernels, per_device(): pl.pallas_call(hand_on, out_shape=results, in_specs=[anywhere] * 3, out_s...  2.58 us

profile of v3, /device:TPU:1, one launch (start us, length us, event | category | flops | bytes accessed | tf_op | source)
XLA Modules:
  0.0 97.1 jit_solution(14630727727975635106)
XLA Ops:
  0.6 93.9 %shard_map.85 = (bf16[256,1536]{1,0:T(8,128)(2,1)}, bf16[256,1536]{1,0:T(8,128)(2,1)}, bf16[2,128,1536]{2,1,0:T(8,128)(2,1)}) custom-call(s32[3]{0:T(128)} %ts_ref.1, bf16[256,1536]{1,0:T(8,128)(2,1)} %bitcast.3, bf16[2,128,1536]{2,1,0:T(8,128)(2,1)} %stale_ref.1, bf16[1536,2304]{1,0:T(8,128)(2,1)} %wqkv_ref.1, bf16[768,1536]{1,0:T(8,128)(2,1)} %wout_ref.1, ...), custom_call_target="tpu_custom_call" | custom-call | flops 8000000000 | bytes 18000000 | tf_op jit(solution)/shard_map/pallas_call | solution.py:466
  94.5 2.6 %shard_map.86 = (bf16[256,1536]{1,0:T(8,128)(2,1)}, bf16[256,1536]{1,0:T(8,128)(2,1)}, bf16[2,128,1536]{2,1,0:T(8,128)(2,1)}) custom-call(bf16[256,1536]{1,0:T(8,128)(2,1)} %get-tuple-element.9.a_ref, bf16[256,1536]{1,0:T(8,128)(2,1)} %get-tuple-element.10.b_ref, bf16[2,128,1536]{2,1,0:T(8,128)(2,1)} %get-tuple-element.11.c_ref), custom_call_target="tpu_custom_call" | custom-call | tf_op jit(solution)/shard_map/pallas_call | solution.py:508

commit v4 on v3

--- a/solution.py
+++ b/solution.py
@@ -229,7 +229,7 @@
         loop(8, send_qt)
         if k == 0:
             send_spatial(0, 1)
-            send_temporal(0, 0, 16)
+            send_temporal(0, 0, 10)
         else:
             send_temporal(1, 8, 8)
 
@@ -323,6 +323,7 @@
             loop(4, attend)
 
         if k + 1 < STEPS:
+            send_temporal(0, 10, 6)
             send_spatial(1, 0)
             send_spatial(1, 1)
 

time: 97.4 us -> 102 us (1.047)
  Pallas kernels: 96.5 us -> 101 us
    pallas_call x1, Pallas kernels: 93.9 us -> 98.3 us  [per_device(): pl.pallas_call(kernel, out_shape=results, in_specs=[pl.BlockSpec(memory_s...]
where the time goes in v4:
time: 102 us; the launch traced here: 101 us
  Pallas kernels  101 us (99%)
    pallas_call x1, Pallas kernels, per_device(): pl.pallas_call(kernel, out_shape=results, in_specs=[pl.BlockSpec(memory_s...  98.3 us
    pallas_call x1, Pallas kernels, per_device(): pl.pallas_call(hand_on, out_shape=results, in_specs=[anywhere] * 3, out_s...  2.58 us

profile of v4, /device:TPU:1, one launch (start us, length us, event | category | flops | bytes accessed | tf_op | source)
XLA Modules:
  0.0 101.5 jit_solution(5383100499188747599)
XLA Ops:
  0.6 98.3 %shard_map.85 = (bf16[256,1536]{1,0:T(8,128)(2,1)}, bf16[256,1536]{1,0:T(8,128)(2,1)}, bf16[2,128,1536]{2,1,0:T(8,128)(2,1)}) custom-call(s32[3]{0:T(128)} %ts_ref.1, bf16[256,1536]{1,0:T(8,128)(2,1)} %bitcast.3, bf16[2,128,1536]{2,1,0:T(8,128)(2,1)} %stale_ref.1, bf16[1536,2304]{1,0:T(8,128)(2,1)} %wqkv_ref.1, bf16[768,1536]{1,0:T(8,128)(2,1)} %wout_ref.1, ...), custom_call_target="tpu_custom_call" | custom-call | flops 8000000000 | bytes 18000000 | tf_op jit(solution)/shard_map/pallas_call | solution.py:467
  98.9 2.6 %shard_map.86 = (bf16[256,1536]{1,0:T(8,128)(2,1)}, bf16[256,1536]{1,0:T(8,128)(2,1)}, bf16[2,128,1536]{2,1,0:T(8,128)(2,1)}) custom-call(bf16[256,1536]{1,0:T(8,128)(2,1)} %get-tuple-element.9.a_ref, bf16[256,1536]{1,0:T(8,128)(2,1)} %get-tuple-element.10.b_ref, bf16[2,128,1536]{2,1,0:T(8,128)(2,1)} %get-tuple-element.11.c_ref), custom_call_target="tpu_custom_call" | custom-call | tf_op jit(solution)/shard_map/pallas_call | solution.py:509
